TPU v7x, 32 devices: a whole 2x2x4 slice. The times are simulated.
32 devices in a mesh: groups: 2 (over x), seq: 16 (over z, y, core).
Axes of the slice: x: 2, y: 2, z: 4, core: 2. Of those that a mesh axis runs over, the one named last changes fastest.
Arguments:
- prompt_kv: bfloat16 [8192, 1024], P(('groups', 'seq')), parts along dimension 0, may hold values from -6 to 6
- prompt_pages: int32 [16], P('groups'), parts along dimension 0, may hold values from 1 to 16, 32 in all
- prompt_slot: int32 [16], P('groups'), parts along dimension 0, may hold values from 0 to 31, as said below
- cache_kv: bfloat16 [256, 2048, 256], P(('groups', 'seq')), parts along dimension 0, may hold values from -6 to 6
- cache_len: int32 [64], P('groups'), parts along dimension 0, may hold values from 1 to 2048
- queries: bfloat16 [64, 4, 8192], P(('groups', 'seq')), parts along dimension 0, may hold values from -72 to 72
- new_kv: bfloat16 [64, 4, 1024], P(('groups', 'seq')), parts along dimension 0, may hold values from -6 to 6
Outputs:
- attended: bfloat16 [64, 4, 8192], P(('groups', 'seq')), parts along dimension 0
There are 2 independent parts, one for each index of `groups`. A program takes and returns all parts, laid end to end along the dimension named above; each array names one. Nothing has to cross between parts.
Inputs may be any that keep to these rules, and one draw needn't show every extreme that they name: `prompt_slot`: distinct decode rows.
All inputs are finite; a program needn't handle non-finite values.
Results may differ from a plain program's by a relative error of at most 0.0061.
Values may be sent and summed in bfloat16 or wider, within the bound.
A program may use at most 128 MiB of HBM per device.

v0:
```python
import jax
import jax.numpy as jnp
from jax import lax
from jax.sharding import PartitionSpec as P

HD = 128
KVH = 4
QPK = 16
PAGE = 128


THETA = 500000.0


def partner(array, axis, bit):
    return lax.ppermute(array, axis, [(i, i ^ 1 << bit) for i in range(lax.axis_size(axis))])


def rotate(keys, positions):
    half = keys.shape[-1] // 2
    freq = THETA ** (-(2.0 * jnp.arange(half, dtype=jnp.float32)) / keys.shape[-1])
    angle = positions.astype(jnp.float32)[:, None] * freq[None, :]
    cosine = jnp.cos(angle)[:, None, :]
    sine = jnp.sin(angle)[:, None, :]
    first = keys[..., :half]
    second = keys[..., half:]
    return jnp.concatenate(
        [first * cosine - second * sine, second * cosine + first * sine], axis=-1
    )


def page_tables(prompt_pages, prompt_slot, npage):
    ends = jnp.cumsum(prompt_pages)
    starts = ends - prompt_pages
    page_ids = jnp.arange(npage, dtype=jnp.int32)
    owner = jnp.sum((page_ids[:, None] >= ends[None, :]).astype(jnp.int32), axis=1)
    onehot = (owner[:, None] == jnp.arange(prompt_pages.shape[0], dtype=jnp.int32)[None, :]).astype(
        jnp.int32
    )
    page_start = jnp.sum(onehot * starts[None, :], axis=1)
    page_slot = jnp.sum(onehot * prompt_slot[None, :], axis=1)
    return (page_start, page_slot)


def block_scores(query, keys, valid):
    scores = jnp.einsum("rsjd,rcd->rsjc", query, keys, preferred_element_type=jnp.float32)
    scores = scores * HD ** (-0.5)
    return jnp.where(valid[:, :, None, :], scores, -jnp.inf)


def block_values(weights, values):
    return jnp.einsum("rsjc,rcd->rsjd", weights, values, preferred_element_type=jnp.float32)


def upper_half(bit):
    return [entry for entry in range(KVH) if (entry >> bit) % 2 == 1]


def per_device(prompt_kv, prompt_pages, prompt_slot, cache_kv, cache_len, queries, new_kv):
    nseq = lax.axis_size("seq")
    me = lax.axis_index("seq")
    tok_dev = prompt_kv.shape[0]
    ppd = tok_dev // PAGE
    npage = ppd * nseq
    rows = cache_kv.shape[0]
    ctx = cache_kv.shape[1]
    groups = nseq // KVH
    per_src = queries.shape[0]
    steps = queries.shape[1]
    grp = me // KVH
    my_head = me % KVH
    order = jnp.bitwise_xor(jnp.arange(KVH, dtype=jnp.int32), my_head)
    levels = KVH.bit_length() - 1
    zero = jnp.zeros((), jnp.bfloat16)
    page_start, page_slot = page_tables(prompt_pages, prompt_slot, npage)
    my_start = lax.dynamic_slice_in_dim(page_start, me * ppd, ppd)
    my_slot = lax.dynamic_slice_in_dim(page_slot, me * ppd, ppd)
    offset = jnp.arange(tok_dev, dtype=jnp.int32)
    positions = (
        me * tok_dev + offset - jnp.repeat(my_start, PAGE, total_repeat_length=tok_dev) * PAGE
    )
    packed = prompt_kv.reshape(tok_dev, KVH, 2 * HD)
    rotated = rotate(packed[:, :, :HD].astype(jnp.float32), positions).astype(jnp.bfloat16)
    handed = jnp.concatenate([rotated, packed[:, :, HD:]], axis=-1)
    by_head = handed.reshape(ppd, PAGE, KVH, 2 * HD).transpose(2, 0, 1, 3)
    keep = jnp.arange(groups, dtype=jnp.int32)[:, None] == (my_slot // rows)[None, :]
    outgoing = jnp.where(keep[:, None, :, None, None], by_head[None], zero).reshape(
        nseq, ppd, PAGE, 2 * HD
    )
    arrived = lax.all_to_all(outgoing, "seq", split_axis=0, concat_axis=0, tiled=True).reshape(
        npage, PAGE * 2 * HD
    )
    q_by_head = queries.reshape(per_src, steps, KVH, QPK * HD)
    kv_by_head = new_kv.reshape(per_src, steps, KVH, 2 * HD)
    joined = jnp.concatenate([q_by_head, kv_by_head], axis=-1).transpose(2, 0, 1, 3)
    outbound = jnp.take(joined, order, axis=0)
    for bit in range(levels):
        upper = upper_half(bit)
        sent = jnp.stack([outbound[entry] for entry in upper])
        landed = partner(sent, "seq", bit)
        pieces = [outbound[entry] for entry in range(KVH)]
        for place, entry in enumerate(upper):
            pieces[entry] = landed[place]
        outbound = jnp.stack(pieces)
    inbound = jnp.take(outbound, order, axis=0).reshape(rows, steps, (QPK + 2) * HD)
    mine_q = inbound[..., : QPK * HD].reshape(rows, steps, QPK, HD)
    mine_kv = inbound[..., QPK * HD :]
    slot_ids = grp * rows + jnp.arange(rows, dtype=jnp.int32)
    match = prompt_slot[None, :] == slot_ids[:, None]
    has = jnp.any(match, axis=1)
    fresh_len = jnp.sum(match.astype(jnp.int32) * prompt_pages[None, :], axis=1) * PAGE
    my_cache_len = lax.dynamic_slice_in_dim(cache_len, grp * rows, rows)
    column = jnp.arange(ctx, dtype=jnp.int32)
    step_ids = jnp.arange(steps, dtype=jnp.int32)
    new_valid = (step_ids[None, :] <= step_ids[:, None])[None]
    new_valid = jnp.broadcast_to(new_valid, (rows, steps, steps))
    page_off = jnp.arange(npage, dtype=jnp.int32) - page_start
    target = (page_slot[None, None, :] == slot_ids[:, None, None]) & (
        page_off[None, None, :] == jnp.arange(ctx // PAGE, dtype=jnp.int32)[None, :, None]
    )
    fresh = jnp.dot(
        target.astype(jnp.bfloat16).reshape(rows * (ctx // PAGE), npage),
        arrived,
        preferred_element_type=jnp.float32,
    )
    fresh = fresh.astype(jnp.bfloat16).reshape(rows, ctx, 2 * HD)
    context = jnp.where(has[:, None, None], fresh, cache_kv)
    length = jnp.where(has, fresh_len, my_cache_len)
    ctx_valid = jnp.broadcast_to(
        (column[None, :] < length[:, None])[:, None, :], (rows, steps, ctx)
    )
    blocks = [(context[..., :HD], context[..., HD:], ctx_valid)]
    blocks = blocks + [(mine_kv[..., :HD], mine_kv[..., HD:], new_valid)]
    scored = [block_scores(mine_q, keys, valid) for keys, values, valid in blocks]
    top = scored[0].max(axis=-1, keepdims=True)
    for scores in scored[1:]:
        top = jnp.maximum(top, scores.max(axis=-1, keepdims=True))
    total = jnp.zeros(top.shape, jnp.float32)
    summed = jnp.zeros((rows, steps, QPK, HD), jnp.float32)
    for scores, block in zip(scored, blocks):
        expo = jnp.exp(scores - top)
        total = total + jnp.sum(expo, axis=-1, keepdims=True)
        summed = summed + block_values(expo.astype(jnp.bfloat16), block[1])
    result = (summed / total).astype(jnp.bfloat16).reshape(KVH, per_src, steps, QPK * HD)
    returning = jnp.take(result, order, axis=0)
    for bit in range(levels):
        upper = upper_half(bit)
        sent = jnp.stack([returning[entry] for entry in upper])
        landed = partner(sent, "seq", bit)
        pieces = [returning[entry] for entry in range(KVH)]
        for place, entry in enumerate(upper):
            pieces[entry] = landed[place]
        returning = jnp.stack(pieces)
    back = jnp.take(returning, order, axis=0)
    return back.transpose(1, 2, 0, 3).reshape(per_src, steps, KVH * QPK * HD)


def solution(mesh):
    placed = (
        P(("groups", "seq"), None),
        P("groups"),
        P("groups"),
        P(("groups", "seq"), None, None),
        P("groups"),
        P(("groups", "seq"), None, None),
        P(("groups", "seq"), None, None),
    )
    return jax.shard_map(
        per_device,
        mesh=mesh,
        in_specs=placed,
        out_specs=P(("groups", "seq"), None, None),
        check_vma=False,
    )
```

profile of v0, /device:TPU:18, one launch (start us, length us, event | category | flops | bytes accessed | tf_op | source)
XLA Modules:
  0.0 102.7 jit_solution(16757115818750427356)
XLA Ops:
  0.0 0.8 reduce-window.12
  0.9 0.7 bitcast_subtract_fusion
  1.6 0.7 select_reduce_fusion.1
  3.0 1.4 %reshape.340 = bf16[256,4,256]{2,1,0:T(4,128)(2,1)S(1)} reshape(bf16[256,1024]{1,0:T(8,128)(2,1)} %param.13) | data formatting | bytes 1048576 | tf_op jit(solution)/shard_map/reshape | solution.py:82
  4.6 1.3 %compare_select_fusion.2 = s32[256,1]{0,1:T(1,128)S(1)} fusion(s32[256,1]{0,1:T(1,128)S(1)} %bitcast.85, s32[256,1]{0,1:T(1,128)S(1)} %bitcast.84, s32[]{:T(128)} %bitcast.11, s32[]{:T(128)} %bitcast.10), kind=kLoop, calls=%fused_computation.63 | loop fusion | flops 1024 | bytes 3080 | tf_op jit(solution)/shard_map/jit(_take)/gather | solution.py:80
  8.0 1.6 %bitcast_select_fusion = bf16[16,2,128,256]{3,2,1,0:T(8,128)(2,1)} fusion(pred[16,2]{1,0:T(8,128)(4,1)S(1)} %bitcast.82, bf16[4,2,128,256]{3,2,1,0:T(8,128)(2,1)S(1)} %copy.22), kind=kLoop, calls=%fused_computation.15 | loop fusion | flops 1048576 | bytes 2621472 | tf_op jit(solution)/shard_map/jit(_where)/select_n | solution.py:87
  9.6 6.2 %all-to-all-start = ((bf16[16,2,128,256]{3,2,1,0:T(8,128)(2,1)}), bf16[16,2,128,256]{3,2,1,0:T(8,128)(2,1)S(1)}, u32[]{:S(2)}, u32[]{:S(2)}) async-start(bf16[16,2,128,256]{3,2,1,0:T(8,128)(2,1)} %bitcast_select_fusion), calls=%async_computation | async-start | bytes 4194304 | tf_op jit(solution)/shard_map/all_to_all | solution.py:90
  16.0 0.7 gather_fusion
  18.3 1.5 %collective-permute-start.1 = (bf16[2,2,4,2304]{3,2,1,0:T(4,128)(2,1)S(1)}, bf16[2,2,4,2304]{3,2,1,0:T(4,128)(2,1)S(1)}, u32[]{:S(2)}, u32[]{:S(2)}) collective-permute-start(bf16[2,2,4,2304]{3,2,1,0:T(4,128)(2,1)S(1)} %pad_maximum_fusion.4), channel_id=1, source_target_pairs={{0,2},{1,3},{2,0},{3,1},{4,6},{5,7},{6,4},{7,5},{8,10},{9,11},{10,... | collective-permute-start | bytes 221192 | tf_op jit(solution)/shard_map/ppermute | solution.py:16
  19.9 11.3 %collective-permute-done.1 = bf16[2,2,4,2304]{3,2,1,0:T(4,128)(2,1)S(1)} collective-permute-done((bf16[2,2,4,2304]{3,2,1,0:T(4,128)(2,1)S(1)}, bf16[2,2,4,2304]{3,2,1,0:T(4,128)(2,1)S(1)}, u32[]{:S(2)}, u32[]{:S(2)}) %collective-permute-start.1) | collective-permute-done | bytes 73760 | tf_op jit(solution)/shard_map/ppermute | solution.py:16
  31.3 0.7 gather_fusion.1
  32.7 30.7 %all-to-all-done = bf16[16,2,128,256]{3,2,1,0:T(8,128)(2,1)S(1)} async-done(((bf16[16,2,128,256]{3,2,1,0:T(8,128)(2,1)}), bf16[16,2,128,256]{3,2,1,0:T(8,128)(2,1)S(1)}, u32[]{:S(2)}, u32[]{:S(2)}) %all-to-all-start) | async-done | bytes 2097184 | tf_op jit(solution)/shard_map/all_to_all | solution.py:90
  63.4 1.2 %copy.33 = bf16[4,8,128,256]{3,1,2,0:T(8,128)(2,1)S(1)} copy(bf16[4,8,128,256]{3,2,1,0:T(8,128)(2,1)S(1)} %bitcast.72) | data formatting | bytes 4194304
  64.6 5.5 %convolution_convert_fusion = bf16[128,32768]{1,0:T(8,128)(2,1)} fusion(pred[128,32]{1,0:T(8,128)(4,1)S(1)} %bitcast.79, bf16[32,32768]{1,0:T(8,128)(2,1)S(1)} %bitcast.71), kind=kOutput, calls=%fused_computation.4 | convolution fusion | flops 272629760 | bytes 10489856 | tf_op jit(solution)/shard_map/dot_general | solution.py:121
  70.2 13.5 %reshape.343 = bf16[8,2048,256]{2,1,0:T(8,128)(2,1)} reshape(bf16[128,32768]{1,0:T(8,128)(2,1)} %convolution_convert_fusion) | data formatting | bytes 16777216 | tf_op jit(solution)/shard_map/reshape | solution.py:126
  83.6 6.5 %broadcast_select_fusion = bf16[8,2048,256]{2,1,0:T(8,128)(2,1)S(1)} fusion(bf16[8,2048,256]{2,1,0:T(8,128)(2,1)} %reshape.343, bf16[8,2048,256]{2,1,0:T(8,128)(2,1)} %param.16, pred[8]{0:T(512)(128)(4,1)S(1)} %compare_reduce_fusion), kind=kLoop, calls=%fused_computation.5 | loop fusion | flops 4194304 | bytes 25165832 | tf_op jit(solution)/shard_map/jit(_where)/select_n | solution.py:127
  90.1 1.7 %fusion.2 = (f32[8,4,16]{2,1,0:T(4,128)S(1)}, f32[8,4,16,2048]{3,2,1,0:T(8,128)S(1)}) fusion(pred[8,2048]{1,0:T(8,128)(4,1)S(1)} %iota_compare_fusion, bf16[8,4,16,128]{3,2,1,0:T(8,128)(2,1)S(1)} %reshape.337, bf16[8,2048,256]{2,1,0:T(8,128)(2,1)S(1)} %broadcast_select_fusion), kind=kOutput, calls=%fused_computation.12 | convolution fusion | flops 271580672 | bytes 8538112 | tf_op jit(solution)/shard_map/rsjd,rcd->rsjc/dot_general | solution.py:46
  91.8 1.1 %fusion.3 = f32[8,4,16]{2,1,0:T(4,128)S(1)} fusion(f32[8,4,16,2048]{3,2,1,0:T(8,128)S(1)} %get-tuple-element.42, f32[8,4,16]{2,1,0:T(4,128)S(1)} %max.8, pred[8,2048]{1,0:T(8,128)(4,1)S(1)} %iota_compare_fusion), kind=kLoop, calls=%fused_computation.13 | loop fusion | flops 4193792 | bytes 4214784 | tf_op jit(solution)/shard_map/reduce_sum | solution.py:142
  92.9 1.1 %fusion = f32[8,4,16,128]{3,2,1,0:T(8,128)S(1)} fusion(bf16[8,2048,256]{2,1,0:T(8,128)(2,1)S(1)} %broadcast_select_fusion, f32[8,4,16,2048]{3,2,1,0:T(8,128)S(1)} %get-tuple-element.42, f32[8,4,16]{2,1,0:T(4,128)S(1)} %max.8, pred[8,2048]{1,0:T(8,128)(4,1)S(1)} %iota_compare_fusion), kind=kOutput, calls=%fused_computation.7 | convolution fusion | flops 272629760 | bytes 8683520 | tf_op jit(solution)/shard_map/rsjc,rcd->rsjd/dot_general | solution.py:52
  94.4 0.7 gather_fusion.2
  95.4 1.2 %collective-permute-done.2 = bf16[2,2,4,2048]{3,2,1,0:T(4,128)(2,1)S(1)} collective-permute-done((bf16[2,2,4,2048]{3,2,1,0:T(4,128)(2,1)S(1)}, bf16[2,2,4,2048]{3,2,1,0:T(4,128)(2,1)S(1)}, u32[]{:S(2)}, u32[]{:S(2)}) %collective-permute-start.2) | collective-permute-done | bytes 65568 | tf_op jit(solution)/shard_map/ppermute | solution.py:16
  96.8 4.3 %collective-permute-done.3 = bf16[2,2,4,2048]{3,2,1,0:T(4,128)(2,1)S(1)} collective-permute-done((bf16[2,2,4,2048]{3,2,1,0:T(4,128)(2,1)S(1)}, bf16[2,2,4,2048]{3,2,1,0:T(4,128)(2,1)S(1)}, u32[]{:S(2)}, u32[]{:S(2)}) %collective-permute-start.3) | collective-permute-done | bytes 65568 | tf_op jit(solution)/shard_map/ppermute | solution.py:16
  101.2 0.7 gather_fusion.3
  102.0 0.7 copy.32
  (68 shorter events, 6.5 us)
Async XLA Ops:
  7.6 8.2 %copy-start = (bf16[2,4,8192]{2,1,0:T(4,128)(2,1)S(1)}, bf16[2,4,8192]{2,1,0:T(4,128)(2,1)}, u32[]{:S(2)}) copy-start(bf16[2,4,8192]{2,1,0:T(4,128)(2,1)} %param.18) | copy-start | bytes 393220
  7.6 8.3 %copy-start.1 = (bf16[2,4,1024]{2,1,0:T(4,128)(2,1)S(1)}, bf16[2,4,1024]{2,1,0:T(4,128)(2,1)}, u32[]{:S(2)}) copy-start(bf16[2,4,1024]{2,1,0:T(4,128)(2,1)} %param.19) | copy-start | bytes 49156
  8.0 9.2 %copy-start.2 = (s32[8]{0:T(128)S(1)}, s32[8]{0:T(128)}, u32[]{:S(2)}) copy-start(s32[8]{0:T(128)} %param.15) | copy-start | bytes 100
  8.0 9.4 %copy-start.4 = (s32[8]{0:T(128)S(1)}, s32[8]{0:T(128)}, u32[]{:S(2)}) copy-start(s32[8]{0:T(128)} %param.14) | copy-start | bytes 100
  8.0 9.5 %copy-start.3 = (s32[32]{0:T(128)S(1)}, s32[32]{0:T(128)}, u32[]{:S(2)}) copy-start(s32[32]{0:T(128)} %param.17) | copy-start | bytes 388
  9.6 53.8 %all-to-all-start = ((bf16[16,2,128,256]{3,2,1,0:T(8,128)(2,1)}), bf16[16,2,128,256]{3,2,1,0:T(8,128)(2,1)S(1)}, u32[]{:S(2)}, u32[]{:S(2)}) async-start(bf16[16,2,128,256]{3,2,1,0:T(8,128)(2,1)} %bitcast_select_fusion), calls=%async_computation | async-start | bytes 4194304 | tf_op jit(solution)/shard_map/all_to_all | solution.py:90
  16.9 1.3 %collective-permute-start = (bf16[2,2,4,2304]{3,2,1,0:T(4,128)(2,1)S(1)}, bf16[2,2,4,2304]{3,2,1,0:T(4,128)(2,1)S(1)}, u32[]{:S(2)}, u32[]{:S(2)}) collective-permute-start(bf16[2,2,4,2304]{3,2,1,0:T(4,128)(2,1)S(1)} %pad_maximum_fusion.3), channel_id=1, source_target_pairs={{0,1},{1,0},{2,3},{3,2},{4,5},{5,4},{6,7},{7,6},{8,9},{9,8},{10,11... | collective-permute-start | bytes 221192 | tf_op jit(solution)/shard_map/ppermute | solution.py:16
  18.3 12.9 %collective-permute-start.1 = (bf16[2,2,4,2304]{3,2,1,0:T(4,128)(2,1)S(1)}, bf16[2,2,4,2304]{3,2,1,0:T(4,128)(2,1)S(1)}, u32[]{:S(2)}, u32[]{:S(2)}) collective-permute-start(bf16[2,2,4,2304]{3,2,1,0:T(4,128)(2,1)S(1)} %pad_maximum_fusion.4), channel_id=1, source_target_pairs={{0,2},{1,3},{2,0},{3,1},{4,6},{5,7},{6,4},{7,5},{8,10},{9,11},{10,... | collective-permute-start | bytes 221192 | tf_op jit(solution)/shard_map/ppermute | solution.py:16
  95.3 1.3 %collective-permute-start.2 = (bf16[2,2,4,2048]{3,2,1,0:T(4,128)(2,1)S(1)}, bf16[2,2,4,2048]{3,2,1,0:T(4,128)(2,1)S(1)}, u32[]{:S(2)}, u32[]{:S(2)}) collective-permute-start(bf16[2,2,4,2048]{3,2,1,0:T(4,128)(2,1)S(1)} %pad_maximum_fusion.5), channel_id=1, source_target_pairs={{0,1},{1,0},{2,3},{3,2},{4,5},{5,4},{6,7},{7,6},{8,9},{9,8},{10,11... | collective-permute-start | bytes 196616 | tf_op jit(solution)/shard_map/ppermute | solution.py:16
  96.8 4.3 %collective-permute-start.3 = (bf16[2,2,4,2048]{3,2,1,0:T(4,128)(2,1)S(1)}, bf16[2,2,4,2048]{3,2,1,0:T(4,128)(2,1)S(1)}, u32[]{:S(2)}, u32[]{:S(2)}) collective-permute-start(bf16[2,2,4,2048]{3,2,1,0:T(4,128)(2,1)S(1)} %pad_maximum_fusion.6), channel_id=1, source_target_pairs={{0,2},{1,3},{2,0},{3,1},{4,6},{5,7},{6,4},{7,5},{8,10},{9,11},{10,... | collective-permute-start | bytes 196616 | tf_op jit(solution)/shard_map/ppermute | solution.py:16
where the time goes:
time: 103 us
  waiting for transfers between devices  48 us (47%)
  local copies, waits for them, and re-layouts  20.8 us (20%)
  other arithmetic  16.5 us (16%)
  matrix products  9.05 us (9%)
  starting transfers between devices  8.07 us (8%)
    all_to_all x1, waiting for transfers between devices, per_device(): lax.all_to_all(outgoing, 'seq', split_axis=0, concat_axis=0, tiled=True)  30.7 us
    ppermute x4, waiting for transfers between devices, partner(): lax.ppermute(array, axis, [(i, i ^ 1 << bit) for i in range(lax.axis_size...  17.3 us
    reshape x1, local copies, waits for them, and re-layouts, per_device(): fresh = fresh.astype(jnp.bfloat16).reshape(rows, ctx, 2 * HD)  13.5 us
    select_n x1, other arithmetic, per_device(): context = jnp.where(has[:, None, None], fresh, cache_kv)  6.5 us
    all_to_all x1, starting transfers between devices, per_device(): lax.all_to_all(outgoing, 'seq', split_axis=0, concat_axis=0, tiled=True)  6.19 us
    dot_general x1, matrix products, per_device(): jnp.dot(target.astype(jnp.bfloat16).reshape(rows * (ctx // PAGE), npage),...  5.54 us
    dot_general x2, matrix products, block_scores(): jnp.einsum('rsjd,rcd->rsjc', query, keys, preferred_element_type=jnp.floa...  2.12 us
  transfers between devices with their start and end apart: 5, of which 5 were waited for; matrix products, arithmetic and copies ran while one was open for 3% of the time, Pallas kernels for 0%

commit v1 on v0

v1 whole, which is shorter than its diff:
```python
import functools

import jax
import jax.numpy as jnp
from jax import lax
from jax.experimental import pallas as pl
from jax.experimental.pallas import tpu as pltpu
from jax.sharding import PartitionSpec as P

HD = 128
KVH = 4
QPK = 16
PAGE = 128
THETA = 500000.0
LOW = -1e30
MESH = pl.DeviceIdType.MESH
BF = jnp.bfloat16
F32 = jnp.float32


def dot_t(a, b):
    return lax.dot_general(a, b, (((1,), (1,)), ((), ())), preferred_element_type=F32)


def dot(a, b):
    return jnp.dot(a, b, preferred_element_type=F32)


def kernel(
    nseq, steps, per_src, ppd, nprompt, ctx,
    pages_ref, slot_ref, clen_ref, freq_ref, joined_ref, pkv_hbm, cache_hbm,
    out_ref,
    prow, pfirst, plast, rowp,
    pkv, cache, keys, stage1, qall, gq, stage2, q2, stage3, r3, lse, fmax, fsum, facc,
    nmax, nsum, nacc, fin, stage4, r4, res6, r6,
    csem, psem, s1, t1, s2, t2, s3, t3, s4, t4, s5, t5, s6, t6,
):
    nslice = KVH * steps
    npage = ppd * nseq
    rows = KVH * per_src
    qrows = nslice * per_src
    qn = steps * QPK
    scale = HD ** -0.5
    me = lax.axis_index("seq")
    grp = me // KVH
    head = me % KVH
    quad = me // nslice
    mine = me % nslice
    step = mine % steps
    qbase = quad * nslice

    barrier = pltpu.get_barrier_semaphore()

    def greet(k, c):
        pl.semaphore_signal(barrier, inc=1, device_id={"seq": (me + k) % nseq}, device_id_type=MESH)
        return c

    lax.fori_loop(1, nseq, greet, 0)

    load_p = pltpu.make_async_copy(pkv_hbm, pkv, psem)
    load_p.start()

    def load_c(r):
        return pltpu.make_async_copy(cache_hbm.at[r], cache.at[r], csem.at[r])

    for r in range(rows):
        load_c(r).start()

    for h in range(KVH):
        for s in range(steps):
            for r in range(per_src):
                stage1[h * steps + s, r, :QPK] = joined_ref[h, r, s * QPK : (s + 1) * QPK]
                stage1[h * steps + s, r, QPK:] = joined_ref[h, r, qn : qn + 16]

    def page_row(g, c):
        p, start, end = c
        new = g >= end
        p = jnp.minimum(jnp.where(new, p + 1, p), nprompt - 1)
        start = jnp.where(new, end, start)
        end = jnp.where(new, end + pages_ref[p], end)
        prow[g] = slot_ref[p]
        pfirst[g] = start
        return p, start, end

    lax.fori_loop(0, npage, page_row, (jnp.int32(0), jnp.int32(0), pages_ref[0]))

    last = jnp.int32(-1)
    for p in range(nprompt):
        last = last + pages_ref[p]
        plast[p] = jnp.clip(last, 0, npage - 1)

    pl.semaphore_wait(barrier, nseq - 1)

    def c1(t, src):
        return pltpu.make_async_remote_copy(
            src_ref=stage1.at[t % nslice], dst_ref=qall.at[pl.ds(src * per_src, per_src)],
            send_sem=s1.at[t], recv_sem=t1.at[src], device_id={"seq": t}, device_id_type=MESH)

    def c2(t, src):
        return pltpu.make_async_remote_copy(
            src_ref=stage2.at[t], dst_ref=q2.at[src],
            send_sem=s2.at[t], recv_sem=t2.at[src], device_id={"seq": qbase + t}, device_id_type=MESH)

    def c3(t, src):
        return pltpu.make_async_remote_copy(
            src_ref=stage3.at[t % nslice], dst_ref=r3.at[src],
            send_sem=s3.at[t], recv_sem=t3.at[src], device_id={"seq": t}, device_id_type=MESH)

    def c4(t, src):
        return pltpu.make_async_remote_copy(
            src_ref=stage4.at[t], dst_ref=r4.at[src],
            send_sem=s4.at[t], recv_sem=t4.at[src], device_id={"seq": qbase + t}, device_id_type=MESH)

    def c5(t, src):
        return pltpu.make_async_remote_copy(
            src_ref=joined_ref.at[t], dst_ref=gq.at[pl.ds(src * per_src, per_src)],
            send_sem=s5.at[t], recv_sem=t5.at[src], device_id={"seq": grp * KVH + t}, device_id_type=MESH)

    def c6(t, src):
        return pltpu.make_async_remote_copy(
            src_ref=res6.at[pl.ds(t * per_src, per_src)], dst_ref=r6.at[src],
            send_sem=s6.at[t], recv_sem=t6.at[src], device_id={"seq": grp * KVH + t}, device_id_type=MESH)

    def send(copy, n, at):
        def go(k, c):
            copy((at + k) % n, at).start()
            return c
        lax.fori_loop(1, n, go, 0)

    def arrive(copy, n, at):
        def go(k, c):
            copy((at + k) % n, (at + n - k) % n).wait_recv()
            return c
        lax.fori_loop(1, n, go, 0)

    def left(copy, n, at):
        def go(k, c):
            copy((at + k) % n, at).wait_send()
            return c
        lax.fori_loop(1, n, go, 0)

    send(c1, nseq, me)
    send(c5, KVH, head)
    qall[pl.ds(me * per_src, per_src)] = stage1[mine]
    gq[pl.ds(head * per_src, per_src)] = joined_ref[head]

    def row_prompt(r, c):
        found = jnp.int32(-1)
        for p in range(nprompt):
            found = jnp.where(slot_ref[p] == r + quad * qrows, p, found)
        rowp[r] = found
        return c

    lax.fori_loop(0, qrows, row_prompt, 0)

    load_p.wait()
    lane = lax.broadcasted_iota(jnp.int32, (PAGE, HD), 1)
    token = lax.broadcasted_iota(jnp.int32, (PAGE, HD), 0)
    for i in range(ppd):
        page = me * ppd + i
        position = (token + (page - pfirst[page]) * PAGE).astype(F32)
        angle = position * freq_ref[0:1, :]
        cosine = jnp.cos(angle)
        sine = jnp.sin(angle)
        sine = jnp.where(lane < HD // 2, -sine, sine)
        for h in range(KVH):
            key = pkv[i * PAGE : (i + 1) * PAGE, h * 2 * HD : h * 2 * HD + HD].astype(F32)
            keys[i, h] = (key * cosine + pltpu.roll(key, HD // 2, 1) * sine).astype(BF)

    arrive(c1, nseq, me)
    for t in range(nslice):
        for i in range(ppd):
            row = prow[(qbase + t) * ppd + i]
            stage2[t, i] = qall[row, :QPK]
    send(c2, nslice, mine)
    q2[mine] = stage2[mine]

    def fresh(tile, valid, q):
        sc = dot_t(q, tile) * scale
        sc = jnp.where(valid, sc, LOW)
        v = pltpu.roll(tile.astype(F32), 16 - steps, 0).astype(BF)
        return sc, v

    col_n = lax.broadcasted_iota(jnp.int32, (QPK, 16), 1)
    for p in range(nprompt):
        row = slot_ref[p]
        tile = qall[row]
        sc, v = fresh(tile[QPK:], col_n <= step, tile[:QPK])
        top = jnp.max(sc, axis=-1, keepdims=True)
        e = jnp.exp(sc - top)
        nmax[p] = jnp.broadcast_to(top, (QPK, HD))
        nsum[p] = jnp.broadcast_to(jnp.sum(e, axis=-1, keepdims=True), (QPK, HD))
        nacc[p] = dot(e.astype(BF), v)

    arrive(c5, KVH, head)
    col_c = lax.broadcasted_iota(jnp.int32, (qn, ctx), 1)
    col_s = lax.broadcasted_iota(jnp.int32, (qn, 16), 1)
    row_s = lax.broadcasted_iota(jnp.int32, (qn, 16), 0) // QPK

    def cached(r, c):
        load_c(r).wait()
        row = grp * rows + r
        length = jnp.where(rowp[row - quad * qrows] >= 0, 0, clen_ref[row])
        tile = gq[r]
        q = tile[:qn]
        sc = dot_t(q, cache[r, :, :HD]) * scale
        sc = jnp.where(col_c < length, sc, LOW)
        sn, v = fresh(tile[qn:], col_s <= row_s, q)
        top = jnp.maximum(jnp.max(sc, axis=-1, keepdims=True), jnp.max(sn, axis=-1, keepdims=True))
        e = jnp.exp(sc - top)
        en = jnp.exp(sn - top)
        total = jnp.sum(e, axis=-1, keepdims=True) + jnp.sum(en, axis=-1, keepdims=True)
        o = dot(e.astype(BF), cache[r, :, HD:]) + dot(en.astype(BF), v)
        res6[r] = (o / total).astype(BF)
        return c

    lax.fori_loop(0, rows // 2, cached, 0)

    arrive(c2, nslice, mine)
    lane_q = lax.broadcasted_iota(jnp.int32, (qn, HD), 1)
    for h in range(KVH):
        packed = jnp.zeros((qn, HD), F32)
        for i in range(ppd):
            q = q2[h * steps : (h + 1) * steps, i].reshape(qn, HD)
            sc = dot_t(q, keys[i, h]) * scale
            top = jnp.max(sc, axis=-1, keepdims=True)
            e = jnp.exp(sc - top)
            total = jnp.sum(e, axis=-1, keepdims=True)
            v = pkv[i * PAGE : (i + 1) * PAGE, h * 2 * HD + HD : (h + 1) * 2 * HD]
            o = dot(e.astype(BF), v) / total
            stage3[h * steps : (h + 1) * steps, i] = o.astype(BF).reshape(steps, QPK, HD)
            x = jnp.broadcast_to(top + jnp.log(total), (qn, HD))
            packed = jnp.where(lane_q // 3 == i, x, packed)
        hi = packed.astype(BF).astype(F32)
        mid = (packed - hi).astype(BF).astype(F32)
        low = packed - hi - mid
        stat = jnp.where(lane_q % 3 == 0, hi, jnp.where(lane_q % 3 == 1, mid, low))
        stage3[h * steps : (h + 1) * steps, ppd] = stat.astype(BF).reshape(steps, QPK, HD)
    send(c3, nseq, me)
    r3[me] = stage3[mine]

    lax.fori_loop(rows // 2, rows, cached, 0)
    send(c6, KVH, head)
    r6[head] = res6[pl.ds(head * per_src, per_src)]

    arrive(c3, nseq, me)
    pick_r = lax.broadcasted_iota(jnp.int32, (HD, ppd * HD), 0)
    pick_c = lax.broadcasted_iota(jnp.int32, (HD, ppd * HD), 1)
    pick = jnp.where(pick_r // 3 == pick_c // HD, 1.0, 0.0).astype(BF)
    lse[...] = dot(r3[:, ppd].reshape(nseq * QPK, HD), pick)

    def at(g):
        return lse[g // ppd * QPK : (g // ppd + 1) * QPK, g % ppd * HD : (g % ppd + 1) * HD]

    opens = [pfirst[g] == g for g in range(npage)]
    drop = [jnp.where(o, F32(LOW), F32(0.0)) for o in opens]
    keep = [jnp.where(o, F32(0.0), F32(1.0)) for o in opens]
    for g in range(npage):
        run = at(g) if g == 0 else jnp.maximum(at(g), run + drop[g])
        fmax[g] = run
    for g in reversed(range(npage)):
        if g < npage - 1:
            run = jnp.maximum(fmax[g], run + drop[g + 1])
        fmax[g] = run
    for g in range(npage):
        w = jnp.exp(at(g) - fmax[g])
        o = r3[g // ppd, g % ppd].astype(F32) * w
        total = w if g == 0 else w + keep[g] * total
        acc = o if g == 0 else o + keep[g] * acc
        fsum[g] = total
        facc[g] = acc
    for p in range(nprompt):
        g = plast[p]
        top = jnp.maximum(fmax[g], nmax[p])
        a = jnp.exp(fmax[g] - top)
        b = jnp.exp(nmax[p] - top)
        fin[p] = ((facc[g] * a + nacc[p] * b) / (fsum[g] * a + nsum[p] * b)).astype(BF)
    for t in range(nslice):
        for i in range(per_src):
            stage4[t, i] = fin[jnp.maximum(rowp[t * per_src + i], 0)]
    send(c4, nslice, mine)
    r4[mine] = stage4[mine]

    arrive(c6, KVH, head)
    arrive(c4, nslice, mine)
    for i in range(per_src):
        has = rowp[mine * per_src + i]
        chosen = jnp.full((QPK, HD), has, jnp.int32) >= 0
        for h in range(KVH):
            for s in range(steps):
                a = r4[h * steps + s, i].astype(F32)
                b = r6[h, i, s * QPK : (s + 1) * QPK].astype(F32)
                out_ref[i, s, h * QPK : (h + 1) * QPK] = jnp.where(chosen, a, b).astype(BF)

    left(c1, nseq, me)
    left(c2, nslice, mine)
    left(c3, nseq, me)
    left(c4, nslice, mine)
    left(c5, KVH, head)
    left(c6, KVH, head)


def per_device(prompt_kv, prompt_pages, prompt_slot, cache_kv, cache_len, queries, new_kv):
    nseq = lax.axis_size("seq")
    tok_dev = prompt_kv.shape[0]
    ppd = tok_dev // PAGE
    npage = ppd * nseq
    rows, ctx = cache_kv.shape[0], cache_kv.shape[1]
    per_src, steps = queries.shape[0], queries.shape[1]
    nprompt = prompt_pages.shape[0]
    nslice = KVH * steps
    qn = steps * QPK

    q = queries.reshape(per_src, steps, KVH, QPK, HD).transpose(2, 0, 1, 3, 4).reshape(KVH, per_src, qn, HD)
    kv = new_kv.reshape(per_src, steps, KVH, 2, HD).transpose(2, 0, 3, 1, 4).reshape(KVH, per_src, 2 * steps, HD)
    joined = jnp.concatenate([q, kv, jnp.zeros((KVH, per_src, 16 - 2 * steps, HD), BF)], axis=2)
    half = HD // 2
    freq = THETA ** (-(2.0 * jnp.arange(half, dtype=F32)) / HD)
    freq = jnp.broadcast_to(jnp.concatenate([freq, freq])[None], (8, HD))

    smem = pl.BlockSpec(memory_space=pltpu.SMEM)
    vmem = pl.BlockSpec(memory_space=pltpu.VMEM)
    hbm = pl.BlockSpec(memory_space=pl.ANY)
    V = pltpu.VMEM
    D = pltpu.SemaphoreType.DMA
    out = pl.pallas_call(
        functools.partial(kernel, nseq, steps, per_src, ppd, nprompt, ctx),
        out_shape=jax.ShapeDtypeStruct((per_src, steps, KVH * QPK, HD), BF),
        in_specs=[smem, smem, smem, vmem, vmem, hbm, hbm],
        out_specs=vmem,
        scratch_shapes=[
            pltpu.SMEM((npage,), jnp.int32),
            pltpu.SMEM((npage,), jnp.int32),
            pltpu.SMEM((nprompt,), jnp.int32),
            pltpu.SMEM((nslice * per_src,), jnp.int32),
            V((tok_dev, KVH * 2 * HD), BF),
            V((rows, ctx, 2 * HD), BF),
            V((ppd, KVH, PAGE, HD), BF),
            V((nslice, per_src, QPK + 16, HD), BF),
            V((nseq * per_src, QPK + 16, HD), BF),
            V((rows, qn + 16, HD), BF),
            V((nslice, ppd, QPK, HD), BF),
            V((nslice, ppd, QPK, HD), BF),
            V((nslice, ppd + 1, QPK, HD), BF),
            V((nseq, ppd + 1, QPK, HD), BF),
            V((nseq * QPK, ppd * HD), F32),
            V((npage, QPK, HD), F32),
            V((npage, QPK, HD), F32),
            V((npage, QPK, HD), F32),
            V((nprompt, QPK, HD), F32),
            V((nprompt, QPK, HD), F32),
            V((nprompt, QPK, HD), F32),
            V((nprompt, QPK, HD), BF),
            V((nslice, per_src, QPK, HD), BF),
            V((nslice, per_src, QPK, HD), BF),
            V((rows, qn, HD), BF),
            V((KVH, per_src, qn, HD), BF),
            D((rows,)),
            D,
            D((nseq,)), D((nseq,)),
            D((nslice,)), D((nslice,)),
            D((nseq,)), D((nseq,)),
            D((nslice,)), D((nslice,)),
            D((KVH,)), D((KVH,)),
            D((KVH,)), D((KVH,)),
        ],
        compiler_params=pltpu.CompilerParams(
            collective_id=0, has_side_effects=True, vmem_limit_bytes=48 * 1024 * 1024
        ),
    )(prompt_pages, prompt_slot, cache_len, freq, joined, prompt_kv, cache_kv)
    return out.reshape(per_src, steps, KVH * QPK * HD)


def solution(mesh):
    placed = (
        P(("groups", "seq"), None),
        P("groups"),
        P("groups"),
        P(("groups", "seq"), None, None),
        P("groups"),
        P(("groups", "seq"), None, None),
        P(("groups", "seq"), None, None),
    )
    return jax.shard_map(
        per_device,
        mesh=mesh,
        in_specs=placed,
        out_specs=P(("groups", "seq"), None, None),
        check_vma=False,
    )
```

time: 103 us -> 41 us (0.40)
  the two profiles are of different devices: /device:TPU:18 before, /device:TPU:0 now
where the time goes in v1:
time: 41 us; the launch traced here: 40.7 us
  Pallas kernels  34.9 us (85%)
  local copies, waits for them, and re-layouts  5.6 us (14%)
    pallas_call x1, Pallas kernels, per_device(): pl.pallas_call(functools.partial(kernel, nseq, steps, per_src, ppd, nprom...  34.9 us
    unnamed x8, local copies, waits for them, and re-layouts  3.01 us
    reshape x2, local copies, waits for them, and re-layouts, per_device(): queries.reshape(per_src, steps, KVH, QPK, HD).transpose(2, 0, 1, 3, 4)  1.07 us

profile of v1, /device:TPU:0, one launch (start us, length us, event | category | flops | bytes accessed | tf_op | source)
XLA Modules:
  0.0 40.7 jit_solution(6434210800760005036)
XLA Ops:
  0.0 1.1 %reshape.16 = bf16[2,4,4,16,128]{4,3,2,1,0:T(8,128)(2,1)S(1)} reshape(bf16[2,4,8192]{2,1,0:T(4,128)(2,1)} %param.12) | data formatting | bytes 262144 | tf_op jit(solution)/shard_map/reshape | solution.py:314
  1.1 0.7 %reshape.18 = bf16[2,4,4,2,128]{4,3,2,1,0:T(2,128)(2,1)S(1)} reshape(bf16[2,4,1024]{2,1,0:T(4,128)(2,1)} %param.13) | data formatting | bytes 32768 | tf_op jit(solution)/shard_map/reshape | solution.py:315
  1.8 0.1 pad.2.clone
  1.9 0.1 maximum_maximum_fusion.joined_ref
  2.0 0.1 pad_maximum_fusion
  2.1 0.0 copy-start
  2.1 1.0 %copy-done = bf16[256,1024]{1,0:T(8,128)(2,1)S(1)} copy-done((bf16[256,1024]{1,0:T(8,128)(2,1)S(1)}, bf16[256,1024]{1,0:T(8,128)(2,1)}, u32[]{:S(2)}) %copy-start) | copy-done | bytes 524312
  3.2 0.0 copy-start.1
  3.2 0.7 %copy-done.1 = s32[8]{0:T(128)S(1)} copy-done((s32[8]{0:T(128)S(1)}, s32[8]{0:T(128)}, u32[]{:S(2)}) %copy-start.1) | copy-done | bytes 56
  3.8 0.0 copy-start.2
  3.8 0.7 %copy-done.2 = s32[8]{0:T(128)S(1)} copy-done((s32[8]{0:T(128)S(1)}, s32[8]{0:T(128)}, u32[]{:S(2)}) %copy-start.2) | copy-done | bytes 56
  4.5 0.0 copy-start.3
  4.5 0.7 %copy-done.3 = s32[32]{0:T(128)S(1)} copy-done((s32[32]{0:T(128)S(1)}, s32[32]{0:T(128)}, u32[]{:S(2)}) %copy-start.3) | copy-done | bytes 152
  5.1 34.9 %shard_map.73 = bf16[2,4,64,128]{3,2,1,0:T(8,128)(2,1)S(1)} custom-call(s32[8]{0:T(128)S(1)} %copy-done.1, s32[8]{0:T(128)S(1)} %copy-done.2, s32[32]{0:T(128)S(1)} %copy-done.3, f32[8,128]{1,0:T(8,128)S(1)} %broadcast_in_dim.4.freq_ref, bf16[4,2,80,128]{3,2,1,0:T(8,128)(2,1)S(1)} %maximum_maximum_fusion.joined_ref, bf16[256,1024]{1,0:T(8,128)(2,1)S(1)} %copy-done, ...), custom_call_target="tpu_custom_call" | custom-call | tf_op jit(solution)/shard_map/pallas_call | solution.py:326
  40.0 0.7 %reshape.20 = bf16[2,4,8192]{2,1,0:T(4,128)(2,1)} reshape(bf16[2,4,64,128]{3,2,1,0:T(8,128)(2,1)S(1)} %shard_map.73) | data formatting | bytes 262144 | tf_op jit(solution)/shard_map/reshape | solution.py:371
  (5 shorter events, 0.0 us)
Async XLA Ops:
  2.1 1.0 %copy-start = (bf16[256,1024]{1,0:T(8,128)(2,1)S(1)}, bf16[256,1024]{1,0:T(8,128)(2,1)}, u32[]{:S(2)}) copy-start(bf16[256,1024]{1,0:T(8,128)(2,1)} %pkv_hbm.1) | copy-start | bytes 1572868
  3.2 0.7 %copy-start.1 = (s32[8]{0:T(128)S(1)}, s32[8]{0:T(128)}, u32[]{:S(2)}) copy-start(s32[8]{0:T(128)} %pages_ref.1) | copy-start | bytes 100
  3.8 0.7 %copy-start.2 = (s32[8]{0:T(128)S(1)}, s32[8]{0:T(128)}, u32[]{:S(2)}) copy-start(s32[8]{0:T(128)} %slot_ref.1) | copy-start | bytes 100
  4.5 0.7 %copy-start.3 = (s32[32]{0:T(128)S(1)}, s32[32]{0:T(128)}, u32[]{:S(2)}) copy-start(s32[32]{0:T(128)} %clen_ref.1) | copy-start | bytes 388

commit v2 on v1

--- a/solution.py
+++ b/solution.py
@@ -28,12 +28,12 @@
 
 def kernel(
     nseq, steps, per_src, ppd, nprompt, ctx,
-    pages_ref, slot_ref, clen_ref, freq_ref, joined_ref, pkv_hbm, cache_hbm,
+    pages_hbm, slot_hbm, clen_hbm, freq_ref, joined_ref, pkv_hbm, cache_hbm,
     out_ref,
-    prow, pfirst, plast, rowp,
-    pkv, cache, keys, stage1, qall, gq, stage2, q2, stage3, r3, lse, fmax, fsum, facc,
+    pages_ref, slot_ref, clen_ref, prow, pfirst, plast, rowp,
+    pkv, cache, keys, stage1, qall, kvall, gq, stage2, q2, stage3, r3, lse, fmax, fsum, facc,
     nmax, nsum, nacc, fin, stage4, r4, res6, r6,
-    csem, psem, s1, t1, s2, t2, s3, t3, s4, t4, s5, t5, s6, t6,
+    csem, psem, isem, s1, t1, s2, t2, s3, t3, s4, t4, s5, t5, s6, t6, s7, t7,
 ):
     nslice = KVH * steps
     npage = ppd * nseq
@@ -57,6 +57,12 @@
 
     lax.fori_loop(1, nseq, greet, 0)
 
+    tables = [
+        pltpu.make_async_copy(a, b, isem.at[n])
+        for n, (a, b) in enumerate([(pages_hbm, pages_ref), (slot_hbm, slot_ref), (clen_hbm, clen_ref)])
+    ]
+    for table in tables:
+        table.start()
     load_p = pltpu.make_async_copy(pkv_hbm, pkv, psem)
     load_p.start()
 
@@ -69,8 +75,10 @@
     for h in range(KVH):
         for s in range(steps):
             for r in range(per_src):
-                stage1[h * steps + s, r, :QPK] = joined_ref[h, r, s * QPK : (s + 1) * QPK]
-                stage1[h * steps + s, r, QPK:] = joined_ref[h, r, qn : qn + 16]
+                stage1[h * steps + s, r] = joined_ref[h, r * qn + s * QPK : r * qn + (s + 1) * QPK]
+
+    for table in tables:
+        table.wait()
 
     def page_row(g, c):
         p, start, end = c
@@ -113,13 +121,18 @@
 
     def c5(t, src):
         return pltpu.make_async_remote_copy(
-            src_ref=joined_ref.at[t], dst_ref=gq.at[pl.ds(src * per_src, per_src)],
+            src_ref=joined_ref.at[t], dst_ref=gq.at[src],
             send_sem=s5.at[t], recv_sem=t5.at[src], device_id={"seq": grp * KVH + t}, device_id_type=MESH)
 
     def c6(t, src):
         return pltpu.make_async_remote_copy(
             src_ref=res6.at[pl.ds(t * per_src, per_src)], dst_ref=r6.at[src],
             send_sem=s6.at[t], recv_sem=t6.at[src], device_id={"seq": grp * KVH + t}, device_id_type=MESH)
+
+    def c7(t, src):
+        return pltpu.make_async_remote_copy(
+            src_ref=joined_ref.at[t % nslice // steps, pl.ds(per_src * qn, 16)], dst_ref=kvall.at[src],
+            send_sem=s7.at[t], recv_sem=t7.at[src], device_id={"seq": t}, device_id_type=MESH)
 
     def send(copy, n, at):
         def go(k, c):
@@ -142,7 +155,7 @@
     send(c1, nseq, me)
     send(c5, KVH, head)
     qall[pl.ds(me * per_src, per_src)] = stage1[mine]
-    gq[pl.ds(head * per_src, per_src)] = joined_ref[head]
+    gq[head] = joined_ref[head]
 
     def row_prompt(r, c):
         found = jnp.int32(-1)
@@ -171,9 +184,11 @@
     for t in range(nslice):
         for i in range(ppd):
             row = prow[(qbase + t) * ppd + i]
-            stage2[t, i] = qall[row, :QPK]
+            stage2[t, i] = qall[row]
     send(c2, nslice, mine)
+    send(c7, nseq, me)
     q2[mine] = stage2[mine]
+    kvall[me] = joined_ref[mine // steps, per_src * qn :]
 
     def fresh(tile, valid, q):
         sc = dot_t(q, tile) * scale
@@ -181,17 +196,6 @@
         v = pltpu.roll(tile.astype(F32), 16 - steps, 0).astype(BF)
         return sc, v
 
-    col_n = lax.broadcasted_iota(jnp.int32, (QPK, 16), 1)
-    for p in range(nprompt):
-        row = slot_ref[p]
-        tile = qall[row]
-        sc, v = fresh(tile[QPK:], col_n <= step, tile[:QPK])
-        top = jnp.max(sc, axis=-1, keepdims=True)
-        e = jnp.exp(sc - top)
-        nmax[p] = jnp.broadcast_to(top, (QPK, HD))
-        nsum[p] = jnp.broadcast_to(jnp.sum(e, axis=-1, keepdims=True), (QPK, HD))
-        nacc[p] = dot(e.astype(BF), v)
-
     arrive(c5, KVH, head)
     col_c = lax.broadcasted_iota(jnp.int32, (qn, ctx), 1)
     col_s = lax.broadcasted_iota(jnp.int32, (qn, 16), 1)
@@ -201,11 +205,12 @@
         load_c(r).wait()
         row = grp * rows + r
         length = jnp.where(rowp[row - quad * qrows] >= 0, 0, clen_ref[row])
-        tile = gq[r]
-        q = tile[:qn]
+        src, turn = r // per_src, r % per_src
+        q = gq[src, pl.ds(pl.multiple_of(turn * qn, qn), qn)]
         sc = dot_t(q, cache[r, :, :HD]) * scale
         sc = jnp.where(col_c < length, sc, LOW)
-        sn, v = fresh(tile[qn:], col_s <= row_s, q)
+        place = col_s - turn * 2 * steps
+        sn, v = fresh(gq[src, per_src * qn :], (place >= 0) & (place <= row_s), q)
         top = jnp.maximum(jnp.max(sc, axis=-1, keepdims=True), jnp.max(sn, axis=-1, keepdims=True))
         e = jnp.exp(sc - top)
         en = jnp.exp(sn - top)
@@ -216,9 +221,12 @@
 
     lax.fori_loop(0, rows // 2, cached, 0)
 
-    arrive(c2, nslice, mine)
     lane_q = lax.broadcasted_iota(jnp.int32, (qn, HD), 1)
     for h in range(KVH):
+        for s in range(steps):
+            @pl.when(h * steps + s != mine)
+            def _():
+                c2(mine, h * steps + s).wait_recv()
         packed = jnp.zeros((qn, HD), F32)
         for i in range(ppd):
             q = q2[h * steps : (h + 1) * steps, i].reshape(qn, HD)
@@ -236,8 +244,25 @@
         low = packed - hi - mid
         stat = jnp.where(lane_q % 3 == 0, hi, jnp.where(lane_q % 3 == 1, mid, low))
         stage3[h * steps : (h + 1) * steps, ppd] = stat.astype(BF).reshape(steps, QPK, HD)
-    send(c3, nseq, me)
+        for block in range(nseq // nslice):
+            for s in range(steps):
+                t = block * nslice + h * steps + s
+                @pl.when(t != me)
+                def _():
+                    c3(t, me).start()
     r3[me] = stage3[mine]
+
+    arrive(c7, nseq, me)
+    col_n = lax.broadcasted_iota(jnp.int32, (QPK, 16), 1)
+    for p in range(nprompt):
+        row = slot_ref[p]
+        place = col_n - row % per_src * 2 * steps
+        sc, v = fresh(kvall[row // per_src], (place >= 0) & (place <= step), qall[row])
+        top = jnp.max(sc, axis=-1, keepdims=True)
+        e = jnp.exp(sc - top)
+        nmax[p] = jnp.broadcast_to(top, (QPK, HD))
+        nsum[p] = jnp.broadcast_to(jnp.sum(e, axis=-1, keepdims=True), (QPK, HD))
+        nacc[p] = dot(e.astype(BF), v)
 
     lax.fori_loop(rows // 2, rows, cached, 0)
     send(c6, KVH, head)
@@ -298,6 +323,7 @@
     left(c4, nslice, mine)
     left(c5, KVH, head)
     left(c6, KVH, head)
+    left(c7, nseq, me)
 
 
 def per_device(prompt_kv, prompt_pages, prompt_slot, cache_kv, cache_len, queries, new_kv):
@@ -311,14 +337,13 @@
     nslice = KVH * steps
     qn = steps * QPK
 
-    q = queries.reshape(per_src, steps, KVH, QPK, HD).transpose(2, 0, 1, 3, 4).reshape(KVH, per_src, qn, HD)
-    kv = new_kv.reshape(per_src, steps, KVH, 2, HD).transpose(2, 0, 3, 1, 4).reshape(KVH, per_src, 2 * steps, HD)
-    joined = jnp.concatenate([q, kv, jnp.zeros((KVH, per_src, 16 - 2 * steps, HD), BF)], axis=2)
+    q = queries.reshape(per_src, steps, KVH, QPK, HD).transpose(2, 0, 1, 3, 4).reshape(KVH, per_src * qn, HD)
+    kv = new_kv.reshape(per_src, steps, KVH, 2, HD).transpose(2, 0, 3, 1, 4).reshape(KVH, per_src * 2 * steps, HD)
+    joined = jnp.concatenate([q, kv], axis=1)
     half = HD // 2
     freq = THETA ** (-(2.0 * jnp.arange(half, dtype=F32)) / HD)
     freq = jnp.broadcast_to(jnp.concatenate([freq, freq])[None], (8, HD))
 
-    smem = pl.BlockSpec(memory_space=pltpu.SMEM)
     vmem = pl.BlockSpec(memory_space=pltpu.VMEM)
     hbm = pl.BlockSpec(memory_space=pl.ANY)
     V = pltpu.VMEM
@@ -326,9 +351,12 @@
     out = pl.pallas_call(
         functools.partial(kernel, nseq, steps, per_src, ppd, nprompt, ctx),
         out_shape=jax.ShapeDtypeStruct((per_src, steps, KVH * QPK, HD), BF),
-        in_specs=[smem, smem, smem, vmem, vmem, hbm, hbm],
+        in_specs=[hbm, hbm, hbm, vmem, vmem, hbm, hbm],
         out_specs=vmem,
         scratch_shapes=[
+            pltpu.SMEM(prompt_pages.shape, jnp.int32),
+            pltpu.SMEM(prompt_slot.shape, jnp.int32),
+            pltpu.SMEM(cache_len.shape, jnp.int32),
             pltpu.SMEM((npage,), jnp.int32),
             pltpu.SMEM((npage,), jnp.int32),
             pltpu.SMEM((nprompt,), jnp.int32),
@@ -336,9 +364,10 @@
             V((tok_dev, KVH * 2 * HD), BF),
             V((rows, ctx, 2 * HD), BF),
             V((ppd, KVH, PAGE, HD), BF),
-            V((nslice, per_src, QPK + 16, HD), BF),
-            V((nseq * per_src, QPK + 16, HD), BF),
-            V((rows, qn + 16, HD), BF),
+            V((nslice, per_src, QPK, HD), BF),
+            V((nseq * per_src, QPK, HD), BF),
+            V((nseq, 16, HD), BF),
+            V((KVH, per_src * qn + 16, HD), BF),
             V((nslice, ppd, QPK, HD), BF),
             V((nslice, ppd, QPK, HD), BF),
             V((nslice, ppd + 1, QPK, HD), BF),
@@ -357,15 +386,17 @@
             V((KVH, per_src, qn, HD), BF),
             D((rows,)),
             D,
+            D((3,)),
             D((nseq,)), D((nseq,)),
             D((nslice,)), D((nslice,)),
             D((nseq,)), D((nseq,)),
             D((nslice,)), D((nslice,)),
             D((KVH,)), D((KVH,)),
             D((KVH,)), D((KVH,)),
+            D((nseq,)), D((nseq,)),
         ],
         compiler_params=pltpu.CompilerParams(
-            collective_id=0, has_side_effects=True, vmem_limit_bytes=48 * 1024 * 1024
+            collective_id=0, has_side_effects=True, vmem_limit_bytes=62 * 1024 * 1024
         ),
     )(prompt_pages, prompt_slot, cache_len, freq, joined, prompt_kv, cache_kv)
     return out.reshape(per_src, steps, KVH * QPK * HD)

time: 41 us -> 36.9 us (0.90)
  Pallas kernels: 34.9 us -> 31.8 us
  local copies, waits for them, and re-layouts: 5.6 us -> 4.01 us
  other arithmetic: 0.19 us -> 0.75 us
    pallas_call x1, Pallas kernels: 34.9 us -> 31.8 us  [per_device(): pl.pallas_call(functools.partial(kernel, nseq, steps, per_src, ppd, nprom...]
    unnamed x8 -> x0, local copies, waits for them, and re-layouts: 3.01 us -> none
    reshape x1, local copies, waits for them, and re-layouts: 0.69 us -> 1.6 us  [per_device(): return out.reshape(per_src, steps, KVH * QPK * HD)]
    broadcast_in_dim x1, local copies, waits for them, and re-layouts: 0.01 us -> 0.6 us  [per_device(): freq = jnp.broadcast_to(jnp.concatenate([freq, freq])[None], (8, HD))]
    concatenate x1, other arithmetic: 0.1 us -> 0.66 us  [per_device(): joined = jnp.concatenate([q, kv], axis=1)]
where the time goes in v2:
time: 36.9 us; the launch traced here: 36.6 us
  Pallas kernels  31.8 us (86%)
  local copies, waits for them, and re-layouts  4.01 us (11%)
  other arithmetic  0.75 us (2%)
    pallas_call x1, Pallas kernels, per_device(): pl.pallas_call(functools.partial(kernel, nseq, steps, per_src, ppd, nprom...  31.8 us
    reshape x1, local copies, waits for them, and re-layouts, per_device(): return out.reshape(per_src, steps, KVH * QPK * HD)  1.6 us
    reshape x2, local copies, waits for them, and re-layouts, per_device(): queries.reshape(per_src, steps, KVH, QPK, HD).transpose(2, 0, 1, 3, 4)  1.07 us
    reshape x2, local copies, waits for them, and re-layouts, per_device(): new_kv.reshape(per_src, steps, KVH, 2, HD).transpose(2, 0, 3, 1, 4)  0.74 us

profile of v2, /device:TPU:0, one launch (start us, length us, event | category | flops | bytes accessed | tf_op | source)
XLA Modules:
  0.0 36.6 jit_solution(7937951998463365211)
XLA Ops:
  0.0 1.1 %reshape.16 = bf16[2,4,4,16,128]{4,3,2,1,0:T(8,128)(2,1)S(1)} reshape(bf16[2,4,8192]{2,1,0:T(4,128)(2,1)} %param.12) | data formatting | bytes 262144 | tf_op jit(solution)/shard_map/reshape | solution.py:340
  1.1 0.7 %reshape.18 = bf16[2,4,4,2,128]{4,3,2,1,0:T(2,128)(2,1)S(1)} reshape(bf16[2,4,1024]{2,1,0:T(4,128)(2,1)} %param.13) | data formatting | bytes 32768 | tf_op jit(solution)/shard_map/reshape | solution.py:341
  1.8 0.7 %pad_maximum_fusion.joined_ref = bf16[4,144,128]{2,1,0:T(8,128)(2,1)} fusion(bf16[4,16,128]{2,1,0:T(8,128)(2,1)S(1)} %bitcast.9, bf16[4,128,128]{2,1,0:T(8,128)(2,1)S(1)} %bitcast.8), kind=kLoop, calls=%fused_computation | loop fusion | flops 294912 | bytes 294912 | tf_op jit(solution)/shard_map/concatenate | solution.py:342
  2.5 0.1 pad_maximum_fusion.1
  2.6 0.6 %broadcast_in_dim.2.freq_ref = f32[8,128]{1,0:T(8,128)} broadcast(f32[128]{0:T(128)S(1)} %pad_maximum_fusion.1), dimensions={1} | broadcast | bytes 4608 | tf_op jit(solution)/shard_map/broadcast_in_dim | solution.py:345
  3.2 31.8 %shard_map.73 = bf16[2,4,64,128]{3,2,1,0:T(8,128)(2,1)} custom-call(s32[8]{0:T(128)} %pages_hbm.1, s32[8]{0:T(128)} %slot_hbm.1, s32[32]{0:T(128)} %clen_hbm.1, f32[8,128]{1,0:T(8,128)} %broadcast_in_dim.2.freq_ref, bf16[4,144,128]{2,1,0:T(8,128)(2,1)} %pad_maximum_fusion.joined_ref, bf16[256,1024]{1,0:T(8,128)(2,1)} %pkv_hbm.1, bf16[8,2048,256]{2,1,0:T(8,128)(2,1)} %cache_hbm.1), custom_call_target="tpu_custom_call" | custom-call | tf_op jit(solution)/shard_map/pallas_call | solution.py:351
  35.0 1.6 %reshape.20 = bf16[2,4,8192]{2,1,0:T(4,128)(2,1)} reshape(bf16[2,4,64,128]{3,2,1,0:T(8,128)(2,1)} %shard_map.73) | data formatting | bytes 262144 | tf_op jit(solution)/shard_map/reshape | solution.py:402
  (3 shorter events, 0.0 us)

commit v3 on v2

--- a/solution.py
+++ b/solution.py
@@ -1,4 +1,5 @@
 import functools
+import math
 
 import jax
 import jax.numpy as jnp
@@ -28,10 +29,10 @@
 
 def kernel(
     nseq, steps, per_src, ppd, nprompt, ctx,
-    pages_hbm, slot_hbm, clen_hbm, freq_ref, joined_ref, pkv_hbm, cache_hbm,
+    pages_hbm, slot_hbm, clen_hbm, q_hbm, kv_hbm, pkv_hbm, cache_hbm,
     out_ref,
     pages_ref, slot_ref, clen_ref, prow, pfirst, plast, rowp,
-    pkv, cache, keys, stage1, qall, kvall, gq, stage2, q2, stage3, r3, lse, fmax, fsum, facc,
+    qin, kvin, kvf, joined_ref, pkv, cache, keys, stage1, qall, kvall, gq, stage2, q2, stage3, r3, lse, fmax, fsum, facc,
     nmax, nsum, nacc, fin, stage4, r4, res6, r6,
     csem, psem, isem, s1, t1, s2, t2, s3, t3, s4, t4, s5, t5, s6, t6, s7, t7,
 ):
@@ -51,34 +52,102 @@
 
     barrier = pltpu.get_barrier_semaphore()
 
-    def greet(k, c):
-        pl.semaphore_signal(barrier, inc=1, device_id={"seq": (me + k) % nseq}, device_id_type=MESH)
-        return c
-
-    lax.fori_loop(1, nseq, greet, 0)
+    def far_first(n):
+        return sorted(range(1, n), key=lambda k: abs(2 * k - n))
+
+    def wrap(t, n):
+        return jnp.where(t >= n, t - n, t)
+
+    def piece(t):
+        return t if nseq == nslice else t % nslice
+
+    for k in far_first(nseq):
+        pl.semaphore_signal(barrier, inc=1, device_id={"seq": wrap(me + k, nseq)}, device_id_type=MESH)
 
     tables = [
         pltpu.make_async_copy(a, b, isem.at[n])
-        for n, (a, b) in enumerate([(pages_hbm, pages_ref), (slot_hbm, slot_ref), (clen_hbm, clen_ref)])
+        for n, (a, b) in enumerate([(pages_hbm, pages_ref), (slot_hbm, slot_ref), (clen_hbm, clen_ref), (q_hbm, qin), (kv_hbm, kvin)])
     ]
     for table in tables:
         table.start()
+    def load_c(r):
+        return pltpu.make_async_copy(cache_hbm.at[r], cache.at[r], csem.at[r])
+
     load_p = pltpu.make_async_copy(pkv_hbm, pkv, psem)
     load_p.start()
-
-    def load_c(r):
-        return pltpu.make_async_copy(cache_hbm.at[r], cache.at[r], csem.at[r])
-
     for r in range(rows):
         load_c(r).start()
-
-    for h in range(KVH):
-        for s in range(steps):
-            for r in range(per_src):
-                stage1[h * steps + s, r] = joined_ref[h, r * qn + s * QPK : r * qn + (s + 1) * QPK]
-
-    for table in tables:
-        table.wait()
+    tables[3].wait()
+    for r in range(per_src):
+        x = qin[r].astype(F32).reshape(steps, KVH * QPK, HD)
+        for h in range(KVH):
+            for s in range(steps):
+                tile = x[s, h * QPK : (h + 1) * QPK].astype(BF)
+                stage1[h * steps + s, r] = tile
+                joined_ref[h, r * qn + s * QPK : r * qn + (s + 1) * QPK] = tile
+
+    pl.semaphore_wait(barrier, nseq - 1)
+
+    def c1(t, src):
+        return pltpu.make_async_remote_copy(
+            src_ref=stage1.at[piece(t)], dst_ref=qall.at[pl.ds(src * per_src, per_src)],
+            send_sem=s1.at[t], recv_sem=t1.at[src], device_id={"seq": t}, device_id_type=MESH)
+
+    def c2(t, src):
+        return pltpu.make_async_remote_copy(
+            src_ref=stage2.at[t], dst_ref=q2.at[src],
+            send_sem=s2.at[t], recv_sem=t2.at[src], device_id={"seq": qbase + t}, device_id_type=MESH)
+
+    def c3(t, src):
+        return pltpu.make_async_remote_copy(
+            src_ref=stage3.at[piece(t)], dst_ref=r3.at[src],
+            send_sem=s3.at[t], recv_sem=t3.at[src], device_id={"seq": t}, device_id_type=MESH)
+
+    def c4(t, src):
+        return pltpu.make_async_remote_copy(
+            src_ref=stage4.at[t], dst_ref=r4.at[src],
+            send_sem=s4.at[t], recv_sem=t4.at[src], device_id={"seq": qbase + t}, device_id_type=MESH)
+
+    def c5(t, src):
+        return pltpu.make_async_remote_copy(
+            src_ref=joined_ref.at[t], dst_ref=gq.at[src],
+            send_sem=s5.at[t], recv_sem=t5.at[src], device_id={"seq": grp * KVH + t}, device_id_type=MESH)
+
+    def c6(t, src):
+        return pltpu.make_async_remote_copy(
+            src_ref=res6.at[pl.ds(t * per_src, per_src)], dst_ref=r6.at[src],
+            send_sem=s6.at[t], recv_sem=t6.at[src], device_id={"seq": grp * KVH + t}, device_id_type=MESH)
+
+    def c7(t, src):
+        return pltpu.make_async_remote_copy(
+            src_ref=joined_ref.at[piece(t) // steps, pl.ds(per_src * qn, 16)], dst_ref=kvall.at[src],
+            send_sem=s7.at[t], recv_sem=t7.at[src], device_id={"seq": t}, device_id_type=MESH)
+
+    def send(copy, n, at):
+        for k in far_first(n):
+            copy(wrap(at + k, n), at).start()
+
+    def arrive(copy, n, at):
+        for k in reversed(far_first(n)):
+            copy(wrap(at + k, n), wrap(at + n - k, n)).wait_recv()
+
+    def left(copy, n, at):
+        for k in far_first(n):
+            copy(wrap(at + k, n), at).wait_send()
+
+    send(c1, nseq, me)
+    for n in (4, 0, 1, 2):
+        tables[n].wait()
+    for r in range(per_src):
+        x = kvin[r].astype(F32)
+        for h in range(KVH):
+            for part in range(2):
+                at = (r * 2 + part) * steps
+                kvf[h, at : at + steps] = x[:, (h * 2 + part) * HD : (h * 2 + part + 1) * HD]
+    joined_ref[:, per_src * qn :] = kvf[...].astype(BF)
+    send(c5, KVH, head)
+    qall[pl.ds(me * per_src, per_src)] = stage1[mine]
+    gq[head] = joined_ref[head]
 
     def page_row(g, c):
         p, start, end = c
@@ -97,66 +166,6 @@
         last = last + pages_ref[p]
         plast[p] = jnp.clip(last, 0, npage - 1)
 
-    pl.semaphore_wait(barrier, nseq - 1)
-
-    def c1(t, src):
-        return pltpu.make_async_remote_copy(
-            src_ref=stage1.at[t % nslice], dst_ref=qall.at[pl.ds(src * per_src, per_src)],
-            send_sem=s1.at[t], recv_sem=t1.at[src], device_id={"seq": t}, device_id_type=MESH)
-
-    def c2(t, src):
-        return pltpu.make_async_remote_copy(
-            src_ref=stage2.at[t], dst_ref=q2.at[src],
-            send_sem=s2.at[t], recv_sem=t2.at[src], device_id={"seq": qbase + t}, device_id_type=MESH)
-
-    def c3(t, src):
-        return pltpu.make_async_remote_copy(
-            src_ref=stage3.at[t % nslice], dst_ref=r3.at[src],
-            send_sem=s3.at[t], recv_sem=t3.at[src], device_id={"seq": t}, device_id_type=MESH)
-
-    def c4(t, src):
-        return pltpu.make_async_remote_copy(
-            src_ref=stage4.at[t], dst_ref=r4.at[src],
-            send_sem=s4.at[t], recv_sem=t4.at[src], device_id={"seq": qbase + t}, device_id_type=MESH)
-
-    def c5(t, src):
-        return pltpu.make_async_remote_copy(
-            src_ref=joined_ref.at[t], dst_ref=gq.at[src],
-            send_sem=s5.at[t], recv_sem=t5.at[src], device_id={"seq": grp * KVH + t}, device_id_type=MESH)
-
-    def c6(t, src):
-        return pltpu.make_async_remote_copy(
-            src_ref=res6.at[pl.ds(t * per_src, per_src)], dst_ref=r6.at[src],
-            send_sem=s6.at[t], recv_sem=t6.at[src], device_id={"seq": grp * KVH + t}, device_id_type=MESH)
-
-    def c7(t, src):
-        return pltpu.make_async_remote_copy(
-            src_ref=joined_ref.at[t % nslice // steps, pl.ds(per_src * qn, 16)], dst_ref=kvall.at[src],
-            send_sem=s7.at[t], recv_sem=t7.at[src], device_id={"seq": t}, device_id_type=MESH)
-
-    def send(copy, n, at):
-        def go(k, c):
-            copy((at + k) % n, at).start()
-            return c
-        lax.fori_loop(1, n, go, 0)
-
-    def arrive(copy, n, at):
-        def go(k, c):
-            copy((at + k) % n, (at + n - k) % n).wait_recv()
-            return c
-        lax.fori_loop(1, n, go, 0)
-
-    def left(copy, n, at):
-        def go(k, c):
-            copy((at + k) % n, at).wait_send()
-            return c
-        lax.fori_loop(1, n, go, 0)
-
-    send(c1, nseq, me)
-    send(c5, KVH, head)
-    qall[pl.ds(me * per_src, per_src)] = stage1[mine]
-    gq[head] = joined_ref[head]
-
     def row_prompt(r, c):
         found = jnp.int32(-1)
         for p in range(nprompt):
@@ -168,11 +177,12 @@
 
     load_p.wait()
     lane = lax.broadcasted_iota(jnp.int32, (PAGE, HD), 1)
+    freq = jnp.exp((lane % (HD // 2)).astype(F32) * (-2.0 * math.log(THETA) / HD))
     token = lax.broadcasted_iota(jnp.int32, (PAGE, HD), 0)
     for i in range(ppd):
         page = me * ppd + i
         position = (token + (page - pfirst[page]) * PAGE).astype(F32)
-        angle = position * freq_ref[0:1, :]
+        angle = position * freq
         cosine = jnp.cos(angle)
         sine = jnp.sin(angle)
         sine = jnp.where(lane < HD // 2, -sine, sine)
@@ -180,13 +190,14 @@
             key = pkv[i * PAGE : (i + 1) * PAGE, h * 2 * HD : h * 2 * HD + HD].astype(F32)
             keys[i, h] = (key * cosine + pltpu.roll(key, HD // 2, 1) * sine).astype(BF)
 
+    send(c7, nseq, me)
+
     arrive(c1, nseq, me)
     for t in range(nslice):
         for i in range(ppd):
             row = prow[(qbase + t) * ppd + i]
             stage2[t, i] = qall[row]
     send(c2, nslice, mine)
-    send(c7, nseq, me)
     q2[mine] = stage2[mine]
     kvall[me] = joined_ref[mine // steps, per_src * qn :]
 
@@ -222,7 +233,7 @@
     lax.fori_loop(0, rows // 2, cached, 0)
 
     lane_q = lax.broadcasted_iota(jnp.int32, (qn, HD), 1)
-    for h in range(KVH):
+    def pages_of(h):
         for s in range(steps):
             @pl.when(h * steps + s != mine)
             def _():
@@ -250,6 +261,12 @@
                 @pl.when(t != me)
                 def _():
                     c3(t, me).start()
+    for plane in range(KVH):
+        @pl.when(mine // steps == plane)
+        def _():
+            for k in (2, 1, 3, 0):
+                pages_of((plane + k) % KVH)
+
     r3[me] = stage3[mine]
 
     arrive(c7, nseq, me)
@@ -337,13 +354,6 @@
     nslice = KVH * steps
     qn = steps * QPK
 
-    q = queries.reshape(per_src, steps, KVH, QPK, HD).transpose(2, 0, 1, 3, 4).reshape(KVH, per_src * qn, HD)
-    kv = new_kv.reshape(per_src, steps, KVH, 2, HD).transpose(2, 0, 3, 1, 4).reshape(KVH, per_src * 2 * steps, HD)
-    joined = jnp.concatenate([q, kv], axis=1)
-    half = HD // 2
-    freq = THETA ** (-(2.0 * jnp.arange(half, dtype=F32)) / HD)
-    freq = jnp.broadcast_to(jnp.concatenate([freq, freq])[None], (8, HD))
-
     vmem = pl.BlockSpec(memory_space=pltpu.VMEM)
     hbm = pl.BlockSpec(memory_space=pl.ANY)
     V = pltpu.VMEM
@@ -351,7 +361,7 @@
     out = pl.pallas_call(
         functools.partial(kernel, nseq, steps, per_src, ppd, nprompt, ctx),
         out_shape=jax.ShapeDtypeStruct((per_src, steps, KVH * QPK, HD), BF),
-        in_specs=[hbm, hbm, hbm, vmem, vmem, hbm, hbm],
+        in_specs=[hbm] * 7,
         out_specs=vmem,
         scratch_shapes=[
             pltpu.SMEM(prompt_pages.shape, jnp.int32),
@@ -361,6 +371,10 @@
             pltpu.SMEM((npage,), jnp.int32),
             pltpu.SMEM((nprompt,), jnp.int32),
             pltpu.SMEM((nslice * per_src,), jnp.int32),
+            V(queries.shape, BF),
+            V(new_kv.shape, BF),
+            V((KVH, 16, HD), F32),
+            V((KVH, per_src * qn + 16, HD), BF),
             V((tok_dev, KVH * 2 * HD), BF),
             V((rows, ctx, 2 * HD), BF),
             V((ppd, KVH, PAGE, HD), BF),
@@ -386,7 +400,7 @@
             V((KVH, per_src, qn, HD), BF),
             D((rows,)),
             D,
-            D((3,)),
+            D((5,)),
             D((nseq,)), D((nseq,)),
             D((nslice,)), D((nslice,)),
             D((nseq,)), D((nseq,)),
@@ -398,7 +412,7 @@
         compiler_params=pltpu.CompilerParams(
             collective_id=0, has_side_effects=True, vmem_limit_bytes=62 * 1024 * 1024
         ),
-    )(prompt_pages, prompt_slot, cache_len, freq, joined, prompt_kv, cache_kv)
+    )(prompt_pages, prompt_slot, cache_len, queries, new_kv, prompt_kv, cache_kv)
     return out.reshape(per_src, steps, KVH * QPK * HD)
 
 

time: 36.9 us -> 33.2 us (0.90)
  local copies, waits for them, and re-layouts: 4.01 us -> 1.6 us
  other arithmetic: 0.75 us -> 0 us
    reshape x4 -> x0, local copies, waits for them, and re-layouts: 1.81 us -> none  [the longest x2 1.07 us: per_device(): queries.reshape(per_src, steps, KVH, QPK, HD).transpose(2, 0, 1, 3, 4)]
    concatenate x2 -> x0, other arithmetic: 0.74 us -> none  [the longest x1 0.66 us: per_device(): joined = jnp.concatenate([q, kv], axis=1)]
    broadcast_in_dim x1 -> x0, local copies, waits for them, and re-layouts: 0.6 us -> none  [per_device(): freq = jnp.broadcast_to(jnp.concatenate([freq, freq])[None], (8, HD))]
where the time goes in v3:
time: 33.2 us; the launch traced here: 33.1 us
  Pallas kernels  31.5 us (95%)
  local copies, waits for them, and re-layouts  1.6 us (5%)
    pallas_call x1, Pallas kernels, per_device(): pl.pallas_call(functools.partial(kernel, nseq, steps, per_src, ppd, nprom...  31.5 us
    reshape x1, local copies, waits for them, and re-layouts, per_device(): return out.reshape(per_src, steps, KVH * QPK * HD)  1.6 us

profile of v3, /device:TPU:0, one launch (start us, length us, event | category | flops | bytes accessed | tf_op | source)
XLA Modules:
  0.0 33.1 jit_solution(13390980799111178857)
XLA Ops:
  0.0 31.5 %shard_map.73 = bf16[2,4,64,128]{3,2,1,0:T(8,128)(2,1)} custom-call(s32[8]{0:T(128)} %pages_hbm.1, s32[8]{0:T(128)} %slot_hbm.1, s32[32]{0:T(128)} %clen_hbm.1, bf16[2,4,8192]{2,1,0:T(4,128)(2,1)} %q_hbm.1, bf16[2,4,1024]{2,1,0:T(4,128)(2,1)} %kv_hbm.1, bf16[256,1024]{1,0:T(8,128)(2,1)} %pkv_hbm.1, bf16[8,2048,256]{2,1,0:T(8,128)(2,1)} %cache_hbm.1), custom_call_target="tpu_custom_call" | custom-call | tf_op jit(solution)/shard_map/pallas_call | solution.py:361
  31.5 1.6 %reshape.3 = bf16[2,4,8192]{2,1,0:T(4,128)(2,1)} reshape(bf16[2,4,64,128]{3,2,1,0:T(8,128)(2,1)} %shard_map.73) | data formatting | bytes 262144 | tf_op jit(solution)/shard_map/reshape | solution.py:416

commit v4 on v3

--- a/solution.py
+++ b/solution.py
@@ -52,8 +52,8 @@
 
     barrier = pltpu.get_barrier_semaphore()
 
-    def far_first(n):
-        return sorted(range(1, n), key=lambda k: abs(2 * k - n))
+    def partners(n):
+        return list(range(1, n))
 
     def wrap(t, n):
         return jnp.where(t >= n, t - n, t)
@@ -61,7 +61,7 @@
     def piece(t):
         return t if nseq == nslice else t % nslice
 
-    for k in far_first(nseq):
+    for k in partners(nseq):
         pl.semaphore_signal(barrier, inc=1, device_id={"seq": wrap(me + k, nseq)}, device_id_type=MESH)
 
     tables = [
@@ -124,15 +124,15 @@
             send_sem=s7.at[t], recv_sem=t7.at[src], device_id={"seq": t}, device_id_type=MESH)
 
     def send(copy, n, at):
-        for k in far_first(n):
+        for k in partners(n):
             copy(wrap(at + k, n), at).start()
 
     def arrive(copy, n, at):
-        for k in reversed(far_first(n)):
+        for k in reversed(partners(n)):
             copy(wrap(at + k, n), wrap(at + n - k, n)).wait_recv()
 
     def left(copy, n, at):
-        for k in far_first(n):
+        for k in partners(n):
             copy(wrap(at + k, n), at).wait_send()
 
     send(c1, nseq, me)

time: 33.2 us -> 32.2 us (0.970)
  Pallas kernels: 31.5 us -> 30.5 us
    pallas_call x1, Pallas kernels: 31.5 us -> 30.5 us  [per_device(): pl.pallas_call(functools.partial(kernel, nseq, steps, per_src, ppd, nprom...]
where the time goes in v4:
time: 32.2 us; the launch traced here: 32.1 us
  Pallas kernels  30.5 us (95%)
  local copies, waits for them, and re-layouts  1.6 us (5%)
    pallas_call x1, Pallas kernels, per_device(): pl.pallas_call(functools.partial(kernel, nseq, steps, per_src, ppd, nprom...  30.5 us
    reshape x1, local copies, waits for them, and re-layouts, per_device(): return out.reshape(per_src, steps, KVH * QPK * HD)  1.6 us

profile of v4, /device:TPU:0, one launch (start us, length us, event | category | flops | bytes accessed | tf_op | source)
XLA Modules:
  0.0 32.1 jit_solution(4641481862531886259)
XLA Ops:
  0.0 30.5 %shard_map.73 = bf16[2,4,64,128]{3,2,1,0:T(8,128)(2,1)} custom-call(s32[8]{0:T(128)} %pages_hbm.1, s32[8]{0:T(128)} %slot_hbm.1, s32[32]{0:T(128)} %clen_hbm.1, bf16[2,4,8192]{2,1,0:T(4,128)(2,1)} %q_hbm.1, bf16[2,4,1024]{2,1,0:T(4,128)(2,1)} %kv_hbm.1, bf16[256,1024]{1,0:T(8,128)(2,1)} %pkv_hbm.1, bf16[8,2048,256]{2,1,0:T(8,128)(2,1)} %cache_hbm.1), custom_call_target="tpu_custom_call" | custom-call | tf_op jit(solution)/shard_map/pallas_call | solution.py:361
  30.5 1.6 %reshape.3 = bf16[2,4,8192]{2,1,0:T(4,128)(2,1)} reshape(bf16[2,4,64,128]{3,2,1,0:T(8,128)(2,1)} %shard_map.73) | data formatting | bytes 262144 | tf_op jit(solution)/shard_map/reshape | solution.py:416
